TPU v7x, 256 devices: a whole 4x4x8 slice. The times are simulated.
256 devices in a mesh: dp: 8 (over y, z_hi), owner: 32 (over x, z_lo, core).
Axes of the slice: x: 4, y: 4, z: 8 (z_hi: 2, z_lo: 4; z = z_hi * 4 + z_lo), core: 2. Of those that a mesh axis runs over, the one named last changes fastest.
Arguments:
- grad_parts: bfloat16 [8, 128, 512, 512], P('dp', None, 'owner'), may hold values from -2.5 to 2.5
- stats: float32 [256, 512, 512], P(('dp', 'owner')), may hold values from -10 to 12, as said below
- roots: bfloat16 [256, 512, 512], P(('dp', 'owner')), may hold values from -0.25 to 0.25
- refresh: int32 [128], P('dp'), may hold values 0 or 1
Outputs:
- new_stats: float32 [256, 512, 512], P(('dp', 'owner'))
- new_roots: bfloat16 [256, 512, 512], P(('dp', 'owner'))
- update: bfloat16 [128, 512, 512], P('dp', 'owner')
Inputs may be any that keep to these rules, and one draw needn't show every extreme that they name: Every stats matrix is symmetric positive definite.
All inputs are finite; a program needn't handle non-finite values. No bound on the sum of `refresh` on one device may be relied on, other than what follows from the above.
Results may differ from a plain program's by a relative error of at most 0.015.
Values may be sent and summed in bfloat16 or wider, within the bound.
A program may use at most 64 MiB of HBM per device.

v0:
```python
import jax
import jax.numpy as jnp
from jax import lax
from jax.sharding import PartitionSpec as P

ITERS = 5
BETA = 0.8


def split_up(x, dim, peers):
    before, after = (x.shape[:dim], x.shape[dim + 1 :])
    return jnp.moveaxis(x.reshape(*before, peers, -1, *after), dim, 0)


def summed_on_arrival(x, axis, dim):
    pieces = split_up(x, dim, lax.axis_size(axis))
    arrived = lax.all_to_all(pieces, axis, split_axis=0, concat_axis=0, tiled=True)
    return arrived.astype(jnp.float32).sum(axis=0)


def partner_2(value, axis, stride):
    mask = 2**stride
    pairs = [(source, source ^ mask) for source in range(lax.axis_size(axis))]
    return lax.ppermute(value, axis, pairs)


def inverse_root(matrix):
    size = matrix.shape[0]
    eye = jnp.eye(size, dtype=jnp.float32)
    scale = jnp.sqrt(jnp.sum(matrix * matrix) + 1e-06)
    current = matrix / scale
    result = eye * scale ** (-0.25)
    for step in range(ITERS):
        factor = (5.0 * eye - current) / 4.0
        result = jnp.dot(result, factor, precision=lax.Precision.HIGHEST)
        if step + 1 < ITERS:
            square = jnp.dot(factor, factor, precision=lax.Precision.HIGHEST)
            fourth = jnp.dot(square, square, precision=lax.Precision.HIGHEST)
            current = jnp.dot(fourth, current, precision=lax.Precision.HIGHEST)
    return result


def local(grad_parts, stats, roots, refresh):
    summed = summed_on_arrival(grad_parts, "dp", 1)
    grad = summed[0].astype(jnp.bfloat16)
    blocks, rows, width = grad.shape
    owner = lax.axis_index("owner")
    side = owner % 2
    flag = lax.dynamic_index_in_dim(refresh, owner // 2, 0, keepdims=False)
    doubled = jnp.repeat(grad, 2, axis=0)
    whole = lax.all_to_all(doubled, "owner", split_axis=0, concat_axis=1, tiled=True)[0]
    oriented = jnp.where(side == 0, whole, whole.T)
    gram = jnp.dot(oriented, oriented.T, preferred_element_type=jnp.float32)
    partner = partner_2(roots, "owner", 0)[0]
    left_root = jnp.where(side == 0, roots[0], partner)
    right_root = jnp.where(side == 0, partner, roots[0])
    product = jnp.dot(left_root, whole, preferred_element_type=jnp.float32).astype(jnp.bfloat16)
    half = width // 2
    right_half = lax.dynamic_slice_in_dim(right_root, side * half, half, 1)
    portion = jnp.dot(product, right_half, preferred_element_type=jnp.float32).astype(jnp.bfloat16)
    moved = lax.all_to_all(portion[None], "owner", split_axis=1, concat_axis=0, tiled=True)
    update = moved.reshape(blocks, 2, rows, half).transpose(0, 2, 1, 3).reshape(blocks, rows, width)
    fresh = BETA * stats[0] + (1.0 - BETA) * (gram / width)
    solved = inverse_root(fresh)
    chosen = jnp.where(flag == 1, solved.astype(jnp.bfloat16), roots[0])
    return (fresh[None], chosen[None], update)


def solution(mesh):
    placed = (
        P("dp", None, "owner", None),
        P(("dp", "owner"), None, None),
        P(("dp", "owner"), None, None),
        P("dp"),
    )
    return jax.shard_map(
        local,
        mesh=mesh,
        in_specs=placed,
        out_specs=(
            P(("dp", "owner"), None, None),
            P(("dp", "owner"), None, None),
            P("dp", "owner", None),
        ),
        check_vma=False,
    )
```

profile of v0, /device:TPU:1, one launch (start us, length us, event | category | flops | bytes accessed | tf_op | source)
XLA Modules:
  0.0 136.4 jit_solution(5005526059796600987)
XLA Ops:
  0.6 47.6 %all_to_all.23 = bf16[8,1,16,16,512]{4,3,2,1,0:T(8,128)(2,1)S(1)} all-to-all(bf16[8,1,16,16,512]{4,3,2,1,0:T(8,128)(2,1)} %bitcast.57), channel_id=1, replica_groups=mesh['dp'=8,'owner'=32] {'dp'}, dimensions={0} | all-to-all | bytes 4194304 | tf_op jit(solution)/shard_map/all_to_all | solution.py:17
  48.2 0.4 reduce_sum.21
  48.6 0.9 broadcast_in_dim.12
  49.4 23.7 %all-to-all-start.1 = ((bf16[32,16,512]{2,1,0:T(8,128)(2,1)}), bf16[32,16,512]{2,1,0:T(8,128)(2,1)S(1)}, u32[]{:S(2)}, u32[]{:S(2)}) async-start(bf16[32,16,512]{2,1,0:T(8,128)(2,1)} %bitcast.2), calls=%async_computation.1 | async-start | bytes 1048576 | tf_op jit(solution)/shard_map/all_to_all | solution.py:51
  73.1 0.3 collective-permute-start
  73.5 0.6 dynamic_slice.7
  74.7 15.2 %all-to-all-done.1 = bf16[32,16,512]{2,1,0:T(8,128)(2,1)S(1)} async-done(((bf16[32,16,512]{2,1,0:T(8,128)(2,1)}), bf16[32,16,512]{2,1,0:T(8,128)(2,1)S(1)}, u32[]{:S(2)}, u32[]{:S(2)}) %all-to-all-start.1) | async-done | bytes 524320 | tf_op jit(solution)/shard_map/all_to_all | solution.py:51
  90.2 1.2 multiply_reduce_fusion
  92.1 1.9 %fusion.6 = bf16[1,512,256]{2,1,0:T(8,128)(2,1)S(1)} fusion(bf16[512,512]{1,0:T(8,128)(2,1)S(1)} %bitcast.55, bf16[1,512,512]{2,1,0:T(8,128)(2,1)} %param.6, bf16[1,512,512]{2,1,0:T(8,128)(2,1)} %collective-permute-done, pred[]{:T(512)S(6)} %eq.26, bf16[512,512]{1,0:T(8,128)(2,1)} %bitcast.61, s32[]{:T(128)S(6)} %select_n.56, bf16[512,512]{1,0:T(8,128)(2,1)} %bitcast.10), kind=kOutput, calls=%fused_computation.14 | convolution fusion | flops 403439616 | bytes 2360832 | tf_op jit(solution)/shard_map/dot_general | solution.py:60
  94.0 0.4 copy.22
  94.5 0.5 broadcast.126
  95.0 2.2 %reduce.2 = bf16[512,256]{1,0:T(8,128)(2,1)S(1)} reduce(bf16[512,1,256]{2,1,0:T(2,128)(2,1)S(1)} %bitcast.58, bf16[]{:T(256)} %broadcast.126), dimensions={1}, to_apply=%bitcast.52.reduce_sub_computation | reduce | bytes 524290
  97.2 0.8 reshape.33
  98.0 3.9 %all-to-all-start.2 = ((bf16[32,2,2048]{2,1,0:T(2,128)(2,1)}), bf16[32,2,2048]{2,1,0:T(2,128)(2,1)S(1)}, u32[]{:S(2)}, u32[]{:S(2)}) async-start(bf16[32,2,2048]{2,1,0:T(2,128)(2,1)} %reshape.33), calls=%async_computation.2 | async-start | bytes 524288 | tf_op jit(solution)/shard_map/all_to_all | solution.py:61
  101.9 2.0 %fusion.25 = f32[512,512]{1,0:T(8,128)S(1)} fusion(f32[512,512]{1,0:T(8,128)S(1)} %get-tuple-element.4, f32[]{:T(128)S(6)} %sqrt.3), kind=kOutput, calls=%fused_computation.29 | convolution fusion | flops 1611923456 | bytes 2097156 | tf_op jit(solution)/shard_map/dot_general | solution.py:37
  103.9 1.9 %fusion.11 = f32[512,512]{1,0:T(8,128)S(1)} fusion(f32[]{:T(128)S(6)} %pow.3, f32[512,512]{1,0:T(8,128)S(1)} %get-tuple-element.4, f32[]{:T(128)S(6)} %sqrt.3), kind=kOutput, calls=%fused_computation.19 | convolution fusion | flops 1612447744 | bytes 2097160 | tf_op jit(solution)/shard_map/dot_general | solution.py:35
  105.8 1.8 %fusion.88 = f32[512,512]{1,0:T(8,128)S(1)} fusion(f32[512,512]{1,0:T(8,128)S(1)} %fusion.25), kind=kOutput, calls=%fused_computation.91 | convolution fusion | flops 1610612736 | bytes 2097152 | tf_op jit(solution)/shard_map/dot_general | solution.py:38
  107.6 1.9 %fusion.87 = f32[512,512]{1,0:T(8,128)S(1)} fusion(f32[512,512]{1,0:T(8,128)S(1)} %fusion.88, f32[512,512]{1,0:T(8,128)S(1)} %get-tuple-element.4, f32[]{:T(128)S(6)} %sqrt.3), kind=kOutput, calls=%fused_computation.89 | convolution fusion | flops 1610874880 | bytes 3145732 | tf_op jit(solution)/shard_map/dot_general | solution.py:39
  109.5 1.9 %fusion.21 = f32[512,512]{1,0:T(8,128)S(1)} fusion(f32[512,512]{1,0:T(8,128)S(1)} %fusion.87), kind=kOutput, calls=%fused_computation.27 | convolution fusion | flops 1611661312 | bytes 2097152 | tf_op jit(solution)/shard_map/dot_general | solution.py:37
  111.4 1.9 %fusion.23 = f32[512,512]{1,0:T(8,128)S(1)} fusion(f32[512,512]{1,0:T(8,128)S(1)} %fusion.11, f32[512,512]{1,0:T(8,128)S(1)} %fusion.87), kind=kOutput, calls=%fused_computation.28 | convolution fusion | flops 1611661312 | bytes 3145728 | tf_op jit(solution)/shard_map/dot_general | solution.py:35
  113.3 1.8 %fusion.89 = f32[512,512]{1,0:T(8,128)S(1)} fusion(f32[512,512]{1,0:T(8,128)S(1)} %fusion.21), kind=kOutput, calls=%fused_computation.92 | convolution fusion | flops 1610612736 | bytes 2097152 | tf_op jit(solution)/shard_map/dot_general | solution.py:38
  115.2 2.1 %fusion.90 = f32[512,512]{1,0:T(8,128)S(1)} fusion(f32[512,512]{1,0:T(8,128)S(1)} %fusion.89, f32[512,512]{1,0:T(8,128)S(1)} %fusion.87), kind=kOutput, calls=%fused_computation.93 | convolution fusion | flops 1610612736 | bytes 3145728 | tf_op jit(solution)/shard_map/dot_general | solution.py:39
  117.3 1.9 %fusion.17 = f32[512,512]{1,0:T(8,128)S(1)} fusion(f32[512,512]{1,0:T(8,128)S(1)} %fusion.90), kind=kOutput, calls=%fused_computation.25 | convolution fusion | flops 1611661312 | bytes 2097152 | tf_op jit(solution)/shard_map/dot_general | solution.py:37
  119.2 1.9 %fusion.19 = f32[512,512]{1,0:T(8,128)S(1)} fusion(f32[512,512]{1,0:T(8,128)S(1)} %fusion.23, f32[512,512]{1,0:T(8,128)S(1)} %fusion.90), kind=kOutput, calls=%fused_computation.26 | convolution fusion | flops 1611661312 | bytes 3145728 | tf_op jit(solution)/shard_map/dot_general | solution.py:35
  121.1 1.8 %fusion.91 = f32[512,512]{1,0:T(8,128)S(1)} fusion(f32[512,512]{1,0:T(8,128)S(1)} %fusion.17), kind=kOutput, calls=%fused_computation.94 | convolution fusion | flops 1610612736 | bytes 2097152 | tf_op jit(solution)/shard_map/dot_general | solution.py:38
  123.0 1.8 %fusion.92 = f32[512,512]{1,0:T(8,128)S(1)} fusion(f32[512,512]{1,0:T(8,128)S(1)} %fusion.91, f32[512,512]{1,0:T(8,128)S(1)} %fusion.90), kind=kOutput, calls=%fused_computation.95 | convolution fusion | flops 1610612736 | bytes 3145728 | tf_op jit(solution)/shard_map/dot_general | solution.py:39
  124.8 1.9 %fusion.13 = f32[512,512]{1,0:T(8,128)S(1)} fusion(f32[512,512]{1,0:T(8,128)S(1)} %fusion.92), kind=kOutput, calls=%fused_computation.23 | convolution fusion | flops 1611661312 | bytes 2097152 | tf_op jit(solution)/shard_map/dot_general | solution.py:37
  126.7 1.9 %fusion.15 = f32[512,512]{1,0:T(8,128)S(1)} fusion(f32[512,512]{1,0:T(8,128)S(1)} %fusion.19, f32[512,512]{1,0:T(8,128)S(1)} %fusion.92), kind=kOutput, calls=%fused_computation.24 | convolution fusion | flops 1611661312 | bytes 3145728 | tf_op jit(solution)/shard_map/dot_general | solution.py:35
  128.7 2.1 %fusion.93 = f32[512,512]{1,0:T(8,128)S(1)} fusion(f32[512,512]{1,0:T(8,128)S(1)} %fusion.13), kind=kOutput, calls=%fused_computation.96 | convolution fusion | flops 1610612736 | bytes 2097152 | tf_op jit(solution)/shard_map/dot_general | solution.py:38
  130.8 1.8 %fusion.1 = f32[512,512]{1,0:T(8,128)S(1)} fusion(f32[512,512]{1,0:T(8,128)S(1)} %fusion.93, f32[512,512]{1,0:T(8,128)S(1)} %fusion.92), kind=kOutput, calls=%fused_computation.7 | convolution fusion | flops 1611661312 | bytes 3145728 | tf_op jit(solution)/shard_map/dot_general | solution.py:39
  132.7 2.7 %fusion.3 = bf16[1,512,512]{2,1,0:T(8,128)(2,1)} fusion(f32[512,512]{1,0:T(8,128)S(1)} %fusion.15, f32[512,512]{1,0:T(8,128)S(1)} %fusion.1, pred[]{:T(512)} %bitcast.6, bf16[1,512,512]{2,1,0:T(8,128)(2,1)S(1)} %copy-done.2), kind=kOutput, calls=%fused_computation.11 | convolution fusion | flops 1611137024 | bytes 3145729 | tf_op jit(solution)/shard_map/dot_general | solution.py:35
  135.6 0.7 copy.20
  (13 shorter events, 0.5 us)
Async XLA Ops:
  48.2 25.3 %copy-start.3 = (s32[16]{0:T(128)S(1)}, s32[16]{0:T(128)}, u32[]{:S(2)}) copy-start(s32[16]{0:T(128)} %param.7) | copy-start | bytes 196
  48.2 42.0 %copy-start = (f32[1,512,512]{2,1,0:T(8,128)S(1)}, f32[1,512,512]{2,1,0:T(8,128)}, u32[]{:S(2)}) copy-start(f32[1,512,512]{2,1,0:T(8,128)} %param.5) | copy-start | bytes 3145732
  49.4 40.5 %all-to-all-start.1 = ((bf16[32,16,512]{2,1,0:T(8,128)(2,1)}), bf16[32,16,512]{2,1,0:T(8,128)(2,1)S(1)}, u32[]{:S(2)}, u32[]{:S(2)}) async-start(bf16[32,16,512]{2,1,0:T(8,128)(2,1)} %bitcast.2), calls=%async_computation.1 | async-start | bytes 1048576 | tf_op jit(solution)/shard_map/all_to_all | solution.py:51
  73.1 19.0 %collective-permute-start = (bf16[1,512,512]{2,1,0:T(8,128)(2,1)}, bf16[1,512,512]{2,1,0:T(8,128)(2,1)}, u32[]{:S(2)}, u32[]{:S(2)}) collective-permute-start(bf16[1,512,512]{2,1,0:T(8,128)(2,1)} %param.6), channel_id=1, source_target_pairs={{0,1},{1,0},{2,3},{3,2},{4,5},{5,4},{6,7},{7,6},{8,9},{9,8},{10,11... | collective-permute-start | bytes 1572872 | tf_op jit(solution)/shard_map/ppermute | solution.py:24
  91.4 16.2 %copy-start.1 = (f32[512,512]{1,0:T(8,128)}, f32[512,512]{1,0:T(8,128)S(1)}, u32[]{:S(2)}) copy-start(f32[512,512]{1,0:T(8,128)S(1)} %get-tuple-element.4) | copy-start | bytes 3145732
  98.0 37.4 %all-to-all-start.2 = ((bf16[32,2,2048]{2,1,0:T(2,128)(2,1)}), bf16[32,2,2048]{2,1,0:T(2,128)(2,1)S(1)}, u32[]{:S(2)}, u32[]{:S(2)}) async-start(bf16[32,2,2048]{2,1,0:T(2,128)(2,1)} %reshape.33), calls=%async_computation.2 | async-start | bytes 524288 | tf_op jit(solution)/shard_map/all_to_all | solution.py:61
  130.8 1.9 %copy-start.2 = (bf16[1,512,512]{2,1,0:T(8,128)(2,1)S(1)}, bf16[1,512,512]{2,1,0:T(8,128)(2,1)}, u32[]{:S(2)}) copy-start(bf16[1,512,512]{2,1,0:T(8,128)(2,1)} %param.6) | copy-start | bytes 1572868
where the time goes:
time: 137 us; the launch traced here: 136 us
  blocking collectives  47.6 us (35%)
  matrix products  36.4 us (27%)
  starting transfers between devices  27.9 us (20%)
  waiting for transfers between devices  15.3 us (11%)
  local copies, waits for them, and re-layouts  4.38 us (3%)
  other arithmetic  2.57 us (2%)
  between operations  2.26 us (2%)
    all_to_all x1, blocking collectives, summed_on_arrival(): lax.all_to_all(pieces, axis, split_axis=0, concat_axis=0, tiled=True)  47.6 us
    all_to_all x1, starting transfers between devices, local(): lax.all_to_all(doubled, 'owner', split_axis=0, concat_axis=1, tiled=True)[0]  23.7 us
    all_to_all x1, waiting for transfers between devices, local(): lax.all_to_all(doubled, 'owner', split_axis=0, concat_axis=1, tiled=True)[0]  15.2 us
    dot_general x5, matrix products, inverse_root(): result = jnp.dot(result, factor, precision=lax.Precision.HIGHEST)  10.3 us
    dot_general x4, matrix products, inverse_root(): square = jnp.dot(factor, factor, precision=lax.Precision.HIGHEST)  7.72 us
    dot_general x4, matrix products, inverse_root(): current = jnp.dot(fourth, current, precision=lax.Precision.HIGHEST)  7.65 us
    dot_general x4, matrix products, inverse_root(): fourth = jnp.dot(square, square, precision=lax.Precision.HIGHEST)  7.63 us
    all_to_all x1, starting transfers between devices, local(): lax.all_to_all(portion[None], 'owner', split_axis=1, concat_axis=0, tiled...  3.85 us
  transfers between devices with their start and end apart: 3, of which 1 were waited for; matrix products, arithmetic and copies ran while one was open for 26% of the time, Pallas kernels for 0%

commit v1 on v0

--- a/solution.py
+++ b/solution.py
@@ -48,7 +48,12 @@
     side = owner % 2
     flag = lax.dynamic_index_in_dim(refresh, owner // 2, 0, keepdims=False)
     doubled = jnp.repeat(grad, 2, axis=0)
-    whole = lax.all_to_all(doubled, "owner", split_axis=0, concat_axis=1, tiled=True)[0]
+    whole = jnp.concatenate(
+        lax.all_to_all(
+            jnp.stack(jnp.split(doubled, lax.axis_size("owner"), axis=0)), "owner", 0, 0
+        ),
+        axis=1,
+    )[0]
     oriented = jnp.where(side == 0, whole, whole.T)
     gram = jnp.dot(oriented, oriented.T, preferred_element_type=jnp.float32)
     partner = partner_2(roots, "owner", 0)[0]

time: 137 us -> 156 us (1.14)
  local copies, waits for them, and re-layouts: 4.38 us -> 23 us
    unnamed x12 -> x41, local copies, waits for them, and re-layouts: 1.61 us -> 20.4 us
  transfers between devices with their start and end apart: 3 -> 3, of which waited for: 1 -> 1; matrix products, arithmetic and copies ran while one was open for 26% -> 23% of each run, Pallas kernels for 0% -> 0%
where the time goes in v1:
time: 156 us
  blocking collectives  47.6 us (31%)
  matrix products  37.5 us (24%)
  starting transfers between devices  27.9 us (18%)
  local copies, waits for them, and re-layouts  23 us (15%)
  waiting for transfers between devices  15.3 us (10%)
  other arithmetic  2.57 us (2%)
  between operations  2.28 us (1%)
    all_to_all x1, blocking collectives, summed_on_arrival(): lax.all_to_all(pieces, axis, split_axis=0, concat_axis=0, tiled=True)  47.6 us
    all_to_all x1, starting transfers between devices, local(): lax.all_to_all(jnp.stack(jnp.split(doubled, lax.axis_size('owner'), axis=...  23.7 us
    unnamed x41, local copies, waits for them, and re-layouts  20.4 us
    all_to_all x1, waiting for transfers between devices, local(): lax.all_to_all(jnp.stack(jnp.split(doubled, lax.axis_size('owner'), axis=...  15.2 us
    dot_general x5, matrix products, inverse_root(): result = jnp.dot(result, factor, precision=lax.Precision.HIGHEST)  11.3 us
    dot_general x4, matrix products, inverse_root(): square = jnp.dot(factor, factor, precision=lax.Precision.HIGHEST)  7.72 us
    dot_general x4, matrix products, inverse_root(): current = jnp.dot(fourth, current, precision=lax.Precision.HIGHEST)  7.65 us
    dot_general x4, matrix products, inverse_root(): fourth = jnp.dot(square, square, precision=lax.Precision.HIGHEST)  7.63 us
  transfers between devices with their start and end apart: 3, of which 1 were waited for; matrix products, arithmetic and copies ran while one was open for 23% of the time, Pallas kernels for 0%

profile of v1, /device:TPU:1, one launch (start us, length us, event | category | flops | bytes accessed | tf_op | source)
XLA Modules:
  0.0 156.0 jit_solution(7133277278637817041)
XLA Ops:
  0.6 47.6 %all_to_all.19 = bf16[8,1,16,16,512]{4,3,2,1,0:T(8,128)(2,1)S(1)} all-to-all(bf16[8,1,16,16,512]{4,3,2,1,0:T(8,128)(2,1)} %bitcast.217), channel_id=1, replica_groups=mesh['dp'=8,'owner'=32] {'dp'}, dimensions={0} | all-to-all | bytes 4194304 | tf_op jit(solution)/shard_map/all_to_all | solution.py:17
  48.6 0.6 constant_dynamic-update-slice_fusion.31
  49.3 0.6 constant_dynamic-update-slice_fusion.30
  49.9 0.6 constant_dynamic-update-slice_fusion.29
  50.5 0.6 constant_dynamic-update-slice_fusion.28
  51.1 0.6 constant_dynamic-update-slice_fusion.27
  51.7 0.6 constant_dynamic-update-slice_fusion.26
  68.1 23.7 %all-to-all-start.1 = ((bf16[32,1,16,512]{3,2,1,0:T(8,128)(2,1)}), bf16[32,1,16,512]{3,2,1,0:T(8,128)(2,1)S(1)}, u32[]{:S(2)}, u32[]{:S(2)}) async-start(bf16[32,1,16,512]{3,2,1,0:T(8,128)(2,1)} %constant_dynamic-update-slice_fusion), calls=%async_computation.1 | async-start | bytes 1048576 | tf_op jit(solution)/shard_map/all_to_all | solution.py:52
  93.3 15.2 %all-to-all-done.1 = bf16[32,1,16,512]{3,2,1,0:T(8,128)(2,1)S(1)} async-done(((bf16[32,1,16,512]{3,2,1,0:T(8,128)(2,1)}), bf16[32,1,16,512]{3,2,1,0:T(8,128)(2,1)S(1)}, u32[]{:S(2)}, u32[]{:S(2)}) %all-to-all-start.1) | async-done | bytes 524320 | tf_op jit(solution)/shard_map/all_to_all | solution.py:52
  108.8 1.2 multiply_reduce_fusion
  110.8 1.9 %fusion.6 = bf16[1,512,256]{2,1,0:T(8,128)(2,1)S(1)} fusion(bf16[512,512]{1,0:T(8,128)(2,1)S(1)} %bitcast.183, bf16[1,512,512]{2,1,0:T(8,128)(2,1)} %param.6, bf16[1,512,512]{2,1,0:T(8,128)(2,1)} %collective-permute-done, pred[]{:T(512)S(6)} %eq.26, bf16[512,512]{1,0:T(8,128)(2,1)} %bitcast.39, s32[]{:T(128)S(6)} %select_n.56, bf16[512,512]{1,0:T(8,128)(2,1)} %bitcast.42), kind=kOutput, calls=%fused_computation.14 | convolution fusion | flops 403439616 | bytes 2360832 | tf_op jit(solution)/shard_map/dot_general | solution.py:65
  113.6 2.2 %reduce.2 = bf16[512,256]{1,0:T(8,128)(2,1)S(1)} reduce(bf16[512,1,256]{2,1,0:T(2,128)(2,1)S(1)} %bitcast.218, bf16[]{:T(256)} %broadcast.126), dimensions={1}, to_apply=%bitcast.180.reduce_sub_computation | reduce | bytes 524290
  115.8 0.8 reshape.29
  116.6 3.9 %all-to-all-start.2 = ((bf16[32,2,2048]{2,1,0:T(2,128)(2,1)}), bf16[32,2,2048]{2,1,0:T(2,128)(2,1)S(1)}, u32[]{:S(2)}, u32[]{:S(2)}) async-start(bf16[32,2,2048]{2,1,0:T(2,128)(2,1)} %reshape.29), calls=%async_computation.2 | async-start | bytes 524288 | tf_op jit(solution)/shard_map/all_to_all | solution.py:66
  120.5 2.0 %fusion.25 = f32[512,512]{1,0:T(8,128)S(1)} fusion(f32[512,512]{1,0:T(8,128)S(1)} %get-tuple-element.4, f32[]{:T(128)S(6)} %sqrt.3), kind=kOutput, calls=%fused_computation.29 | convolution fusion | flops 1611923456 | bytes 2097156 | tf_op jit(solution)/shard_map/dot_general | solution.py:37
  122.5 1.9 %fusion.11 = f32[512,512]{1,0:T(8,128)S(1)} fusion(f32[]{:T(128)S(6)} %pow.3, f32[512,512]{1,0:T(8,128)S(1)} %get-tuple-element.4, f32[]{:T(128)S(6)} %sqrt.3), kind=kOutput, calls=%fused_computation.19 | convolution fusion | flops 1612447744 | bytes 2097160 | tf_op jit(solution)/shard_map/dot_general | solution.py:35
  124.4 1.8 %fusion.88 = f32[512,512]{1,0:T(8,128)S(1)} fusion(f32[512,512]{1,0:T(8,128)S(1)} %fusion.25), kind=kOutput, calls=%fused_computation.155 | convolution fusion | flops 1610612736 | bytes 2097152 | tf_op jit(solution)/shard_map/dot_general | solution.py:38
  126.3 1.9 %fusion.87 = f32[512,512]{1,0:T(8,128)S(1)} fusion(f32[512,512]{1,0:T(8,128)S(1)} %fusion.88, f32[512,512]{1,0:T(8,128)S(1)} %get-tuple-element.4, f32[]{:T(128)S(6)} %sqrt.3), kind=kOutput, calls=%fused_computation.153 | convolution fusion | flops 1610874880 | bytes 3145732 | tf_op jit(solution)/shard_map/dot_general | solution.py:39
  128.1 1.9 %fusion.21 = f32[512,512]{1,0:T(8,128)S(1)} fusion(f32[512,512]{1,0:T(8,128)S(1)} %fusion.87), kind=kOutput, calls=%fused_computation.27 | convolution fusion | flops 1611661312 | bytes 2097152 | tf_op jit(solution)/shard_map/dot_general | solution.py:37
  130.1 1.9 %fusion.23 = f32[512,512]{1,0:T(8,128)S(1)} fusion(f32[512,512]{1,0:T(8,128)S(1)} %fusion.11, f32[512,512]{1,0:T(8,128)S(1)} %fusion.87), kind=kOutput, calls=%fused_computation.28 | convolution fusion | flops 1611661312 | bytes 3145728 | tf_op jit(solution)/shard_map/dot_general | solution.py:35
  132.0 1.8 %fusion.89 = f32[512,512]{1,0:T(8,128)S(1)} fusion(f32[512,512]{1,0:T(8,128)S(1)} %fusion.21), kind=kOutput, calls=%fused_computation.156 | convolution fusion | flops 1610612736 | bytes 2097152 | tf_op jit(solution)/shard_map/dot_general | solution.py:38
  133.8 2.1 %fusion.90 = f32[512,512]{1,0:T(8,128)S(1)} fusion(f32[512,512]{1,0:T(8,128)S(1)} %fusion.89, f32[512,512]{1,0:T(8,128)S(1)} %fusion.87), kind=kOutput, calls=%fused_computation.157 | convolution fusion | flops 1610612736 | bytes 3145728 | tf_op jit(solution)/shard_map/dot_general | solution.py:39
  135.9 1.9 %fusion.17 = f32[512,512]{1,0:T(8,128)S(1)} fusion(f32[512,512]{1,0:T(8,128)S(1)} %fusion.90), kind=kOutput, calls=%fused_computation.25 | convolution fusion | flops 1611661312 | bytes 2097152 | tf_op jit(solution)/shard_map/dot_general | solution.py:37
  137.8 1.9 %fusion.19 = f32[512,512]{1,0:T(8,128)S(1)} fusion(f32[512,512]{1,0:T(8,128)S(1)} %fusion.23, f32[512,512]{1,0:T(8,128)S(1)} %fusion.90), kind=kOutput, calls=%fused_computation.26 | convolution fusion | flops 1611661312 | bytes 3145728 | tf_op jit(solution)/shard_map/dot_general | solution.py:35
  139.7 1.8 %fusion.91 = f32[512,512]{1,0:T(8,128)S(1)} fusion(f32[512,512]{1,0:T(8,128)S(1)} %fusion.17), kind=kOutput, calls=%fused_computation.158 | convolution fusion | flops 1610612736 | bytes 2097152 | tf_op jit(solution)/shard_map/dot_general | solution.py:38
  141.6 1.8 %fusion.92 = f32[512,512]{1,0:T(8,128)S(1)} fusion(f32[512,512]{1,0:T(8,128)S(1)} %fusion.91, f32[512,512]{1,0:T(8,128)S(1)} %fusion.90), kind=kOutput, calls=%fused_computation.159 | convolution fusion | flops 1610612736 | bytes 3145728 | tf_op jit(solution)/shard_map/dot_general | solution.py:39
  143.5 1.9 %fusion.13 = f32[512,512]{1,0:T(8,128)S(1)} fusion(f32[512,512]{1,0:T(8,128)S(1)} %fusion.92), kind=kOutput, calls=%fused_computation.23 | convolution fusion | flops 1611661312 | bytes 2097152 | tf_op jit(solution)/shard_map/dot_general | solution.py:37
  145.4 1.9 %fusion.15 = f32[512,512]{1,0:T(8,128)S(1)} fusion(f32[512,512]{1,0:T(8,128)S(1)} %fusion.19, f32[512,512]{1,0:T(8,128)S(1)} %fusion.92), kind=kOutput, calls=%fused_computation.24 | convolution fusion | flops 1611661312 | bytes 3145728 | tf_op jit(solution)/shard_map/dot_general | solution.py:35
  147.3 2.1 %fusion.93 = f32[512,512]{1,0:T(8,128)S(1)} fusion(f32[512,512]{1,0:T(8,128)S(1)} %fusion.13), kind=kOutput, calls=%fused_computation.160 | convolution fusion | flops 1610612736 | bytes 2097152 | tf_op jit(solution)/shard_map/dot_general | solution.py:38
  149.4 1.9 %fusion.1 = f32[512,512]{1,0:T(8,128)S(1)} fusion(f32[512,512]{1,0:T(8,128)S(1)} %fusion.93, f32[512,512]{1,0:T(8,128)S(1)} %fusion.92), kind=kOutput, calls=%fused_computation.7 | convolution fusion | flops 1611661312 | bytes 3145728 | tf_op jit(solution)/shard_map/dot_general | solution.py:39
  151.3 3.7 %fusion.3 = bf16[1,512,512]{2,1,0:T(8,128)(2,1)} fusion(f32[512,512]{1,0:T(8,128)S(1)} %fusion.15, f32[512,512]{1,0:T(8,128)S(1)} %fusion.1, pred[]{:T(512)} %bitcast.38, bf16[1,512,512]{2,1,0:T(8,128)(2,1)} %param.6), kind=kOutput, calls=%fused_computation.11 | convolution fusion | flops 1611137024 | bytes 3145729 | tf_op jit(solution)/shard_map/dot_general | solution.py:35
  155.3 0.7 copy.51
  (43 shorter events, 18.5 us)
Async XLA Ops:
  48.2 43.9 %copy-start.2 = (s32[16]{0:T(128)S(1)}, s32[16]{0:T(128)}, u32[]{:S(2)}) copy-start(s32[16]{0:T(128)} %param.7) | copy-start | bytes 196
  48.6 60.2 %copy-start = (f32[1,512,512]{2,1,0:T(8,128)S(1)}, f32[1,512,512]{2,1,0:T(8,128)}, u32[]{:S(2)}) copy-start(f32[1,512,512]{2,1,0:T(8,128)} %param.5) | copy-start | bytes 3145732
  68.1 40.5 %all-to-all-start.1 = ((bf16[32,1,16,512]{3,2,1,0:T(8,128)(2,1)}), bf16[32,1,16,512]{3,2,1,0:T(8,128)(2,1)S(1)}, u32[]{:S(2)}, u32[]{:S(2)}) async-start(bf16[32,1,16,512]{3,2,1,0:T(8,128)(2,1)} %constant_dynamic-update-slice_fusion), calls=%async_computation.1 | async-start | bytes 1048576 | tf_op jit(solution)/shard_map/all_to_all | solution.py:52
  91.8 19.0 %collective-permute-start = (bf16[1,512,512]{2,1,0:T(8,128)(2,1)}, bf16[1,512,512]{2,1,0:T(8,128)(2,1)}, u32[]{:S(2)}, u32[]{:S(2)}) collective-permute-start(bf16[1,512,512]{2,1,0:T(8,128)(2,1)} %param.6), channel_id=1, source_target_pairs={{0,1},{1,0},{2,3},{3,2},{4,5},{5,4},{6,7},{7,6},{8,9},{9,8},{10,11... | collective-permute-start | bytes 1572872 | tf_op jit(solution)/shard_map/ppermute | solution.py:24
  110.1 16.2 %copy-start.1 = (f32[512,512]{1,0:T(8,128)}, f32[512,512]{1,0:T(8,128)S(1)}, u32[]{:S(2)}) copy-start(f32[512,512]{1,0:T(8,128)S(1)} %get-tuple-element.4) | copy-start | bytes 3145732
  116.6 38.4 %all-to-all-start.2 = ((bf16[32,2,2048]{2,1,0:T(2,128)(2,1)}), bf16[32,2,2048]{2,1,0:T(2,128)(2,1)S(1)}, u32[]{:S(2)}, u32[]{:S(2)}) async-start(bf16[32,2,2048]{2,1,0:T(2,128)(2,1)} %reshape.29), calls=%async_computation.2 | async-start | bytes 524288 | tf_op jit(solution)/shard_map/all_to_all | solution.py:66
